TPU v7x, 512 devices: a whole 4x4x16 slice. The times are simulated.
512 devices in a mesh: shot: 2 (over core), tx: 8 (over z_hi, y), ty: 32 (over z_lo, x).
Axes of the slice: x: 4, y: 4, z: 16 (z_hi: 2, z_lo: 8; z = z_hi * 8 + z_lo), core: 2. Of those that a mesh axis runs over, the one named last changes fastest.
Arguments:
- forward_fields: float32 [2, 9, 128, 512, 128], P('shot', None, 'tx', 'ty'), may hold values from -6 to 6
- adjoint_fields: float32 [2, 9, 128, 512, 128], P('shot', None, 'tx', 'ty'), may hold values from -6 to 6
- lame_lambda: float32 [128, 512, 128], P('tx', 'ty'), may hold values from 1 to 4
- shear_modulus: float32 [128, 512, 128], P('tx', 'ty'), may hold values from 0.5 to 2
- density: float32 [128, 512, 128], P('tx', 'ty'), may hold values from 1 to 3
- source_cell: int32 [2], P('shot'), may hold values from 0 to 8388607
- source_amp: float32 [2], P('shot'), may hold values from 4 to 12
- receiver_cell: int32 [2, 256], P('shot'), may hold values from 0 to 8388607
- residual_amp: float32 [2, 256], P('shot'), may hold values from -16 to 16
Outputs:
- forward_next: float32 [2, 9, 128, 512, 128], P('shot', None, 'tx', 'ty')
- adjoint_next: float32 [2, 9, 128, 512, 128], P('shot', None, 'tx', 'ty')
- gradient: float32 [3, 128, 512, 128], P(None, 'tx', 'ty')
Inputs may be any that keep to these rules, and one draw needn't show every extreme that they name: `source_cell`: each value is a flat index x * 512 * 128 + y * 128 + z of a grid cell. `receiver_cell`: each value is a flat index x * 512 * 128 + y * 128 + z of a grid cell; receivers may share cells.
All inputs are finite; a program needn't handle non-finite values.
Results may differ from a plain program's by a relative error of at most 0.0001.
Values sent between devices are 32-bit elements; how exact they have to be, the bound alone decides.
A program may use at most 64 MiB of HBM per device.

v0:
```python
import jax
import jax.numpy as jnp
from jax import lax
from jax.sharding import PartitionSpec as P

near_coef = 9.0 / 8.0
far_coef = -1.0 / 24.0
time_step = 0.15


def extended(value, sides, width):
    for axis, dim in sides:
        peers, length = (lax.axis_size(axis), value.shape[dim])
        up = [(i, (i + 1) % peers) for i in range(peers - 1)]
        down = [(j, i) for i, j in up]
        last = lax.slice_in_dim(value, length - width, length, axis=dim)
        initial = lax.slice_in_dim(value, 0, width, axis=dim)
        before = lax.ppermute(last, axis, up)
        after = lax.ppermute(initial, axis, down)
        value = jnp.concatenate([before, value, after], axis=dim)
    return value


def shifted(padded, margin, rim_width, direction, offset):
    rank_count = padded.ndim
    sliced = padded
    for which in range(3):
        length = padded.shape[rank_count - 3 + which] - 2 * margin[which] + 2 * rim_width[which]
        begin_at = margin[which] - rim_width[which] + (offset if which == direction else 0)
        sliced = lax.slice_in_dim(sliced, begin_at, begin_at + length, axis=rank_count - 3 + which)
    return sliced


def depth_table(depth_cells, upward):
    source_row = lax.broadcasted_iota(jnp.int32, (depth_cells, depth_cells), 0)
    target_col = lax.broadcasted_iota(jnp.int32, (depth_cells, depth_cells), 1)
    gap = source_row - target_col
    if upward:
        table = near_coef * (
            (gap == 1).astype(jnp.float32) - (gap == 0).astype(jnp.float32)
        ) + far_coef * ((gap == 2).astype(jnp.float32) - (gap == -1).astype(jnp.float32))
    else:
        table = near_coef * (
            (gap == 0).astype(jnp.float32) - (gap == -1).astype(jnp.float32)
        ) + far_coef * ((gap == 1).astype(jnp.float32) - (gap == -2).astype(jnp.float32))
    return table


def derive(padded, margin, rim_width, direction, upward):
    if direction == 2:
        core = shifted(padded, margin, rim_width, 2, 0)
        return jnp.einsum(
            "...k,ki->...i",
            core,
            depth_table(core.shape[-1], upward),
            precision=lax.Precision.HIGHEST,
        )
    if upward:
        return near_coef * (
            shifted(padded, margin, rim_width, direction, 1)
            - shifted(padded, margin, rim_width, direction, 0)
        ) + far_coef * (
            shifted(padded, margin, rim_width, direction, 2)
            - shifted(padded, margin, rim_width, direction, -1)
        )
    return near_coef * (
        shifted(padded, margin, rim_width, direction, 0)
        - shifted(padded, margin, rim_width, direction, -1)
    ) + far_coef * (
        shifted(padded, margin, rim_width, direction, 1)
        - shifted(padded, margin, rim_width, direction, -2)
    )


def accelerate(stress_ext, buoyancy, margin, rim_width):
    comps = [stress_ext[..., which, :, :, :] for which in range(6)]
    accel_x = (
        derive(comps[0], margin, rim_width, 0, True)
        + derive(comps[3], margin, rim_width, 1, False)
        + derive(comps[4], margin, rim_width, 2, False)
    )
    accel_y = (
        derive(comps[3], margin, rim_width, 0, False)
        + derive(comps[1], margin, rim_width, 1, True)
        + derive(comps[5], margin, rim_width, 2, False)
    )
    accel_z = (
        derive(comps[4], margin, rim_width, 0, False)
        + derive(comps[5], margin, rim_width, 1, False)
        + derive(comps[2], margin, rim_width, 2, True)
    )
    return jnp.stack([accel_x, accel_y, accel_z], axis=-4) * buoyancy


def strain_rates(velocity_ext, margin):
    flat_rim = (0, 0, 0)
    comps = [velocity_ext[..., which, :, :, :] for which in range(3)]
    return jnp.stack(
        [
            derive(comps[0], margin, flat_rim, 0, False),
            derive(comps[1], margin, flat_rim, 1, False),
            derive(comps[2], margin, flat_rim, 2, False),
            derive(comps[0], margin, flat_rim, 1, True)
            + derive(comps[1], margin, flat_rim, 0, True),
            derive(comps[0], margin, flat_rim, 2, True)
            + derive(comps[2], margin, flat_rim, 0, True),
            derive(comps[1], margin, flat_rim, 2, True)
            + derive(comps[2], margin, flat_rim, 1, True),
        ],
        axis=-4,
    )


def new_stress(stress_now, strain, lame_lambda, shear_modulus):
    trace = strain[..., 0, :, :, :] + strain[..., 1, :, :, :] + strain[..., 2, :, :, :]
    normal = stress_now[..., :3, :, :, :] + time_step * (
        lame_lambda * trace[..., None, :, :, :] + 2.0 * shear_modulus * strain[..., :3, :, :, :]
    )
    shear = stress_now[..., 3:, :, :, :] + time_step * shear_modulus * strain[..., 3:, :, :, :]
    return jnp.concatenate([normal, shear], axis=-4)


def image_terms(strain_fwd, stress_adj, accel_fwd, velocity_adj):
    trace_fwd = (
        strain_fwd[..., 0, :, :, :] + strain_fwd[..., 1, :, :, :] + strain_fwd[..., 2, :, :, :]
    )
    trace_adj = (
        stress_adj[..., 0, :, :, :] + stress_adj[..., 1, :, :, :] + stress_adj[..., 2, :, :, :]
    )
    grad_lambda = -time_step * trace_fwd * trace_adj
    grad_shear = -time_step * jnp.sum(strain_fwd * stress_adj, axis=-4)
    grad_density = -time_step * jnp.sum(accel_fwd * velocity_adj, axis=-4)
    return jnp.stack([grad_lambda, grad_shear, grad_density], axis=-4)


def localize(cell_index, x_start, y_start, tile_x, tile_y, width_y, depth_cells):
    plane_size = width_y * depth_cells
    global_x = cell_index // plane_size
    remainder = cell_index % plane_size
    global_y = remainder // depth_cells
    global_z = remainder % depth_cells
    local_x = global_x - x_start
    local_y = global_y - y_start
    inside = (local_x >= 0) & (local_x < tile_x) & (local_y >= 0) & (local_y < tile_y)
    return jnp.where(
        inside, (local_x * tile_y + local_y) * depth_cells + global_z, tile_x * tile_y * depth_cells
    )


def inject(fields, where_cells, amounts):
    field_count, tile_x, tile_y, depth_cells = fields.shape
    column_count = tile_x * tile_y
    column = where_cells // depth_cells
    depth = where_cells % depth_cells
    column_hot = (column[:, None] == lax.broadcasted_iota(jnp.int32, (1, column_count), 1)).astype(
        jnp.float32
    )
    depth_hot = (depth[:, None] == lax.broadcasted_iota(jnp.int32, (1, depth_cells), 1)).astype(
        jnp.float32
    ) * amounts[:, None]
    added = jnp.dot(
        column_hot.T, depth_hot, precision=lax.Precision.HIGHEST, preferred_element_type=jnp.float32
    )
    added = added.reshape(1, tile_x, tile_y, depth_cells)
    return jnp.concatenate([fields[:3], fields[3:6] + added, fields[6:]], axis=0)


def body(
    forward_fields,
    adjoint_fields,
    lame_lambda,
    shear_modulus,
    density,
    source_cell,
    source_amp,
    receiver_cell,
    residual_amp,
):
    shot_count, field_count, tile_x, tile_y, depth_cells = forward_fields.shape
    width_y = tile_y * lax.axis_size("ty")
    x_start = lax.axis_index("tx") * tile_x
    y_start = lax.axis_index("ty") * tile_y
    source_local = localize(source_cell, x_start, y_start, tile_x, tile_y, width_y, depth_cells)
    receiver_local = localize(receiver_cell, x_start, y_start, tile_x, tile_y, width_y, depth_cells)
    forward = jax.vmap(inject)(forward_fields, source_local[:, None], source_amp[:, None])
    adjoint = jax.vmap(inject)(adjoint_fields, receiver_local, residual_amp)
    wavefields = jnp.concatenate([forward, adjoint], axis=0)
    buoyancy = 1.0 / density
    margin = (2, 2, 0)
    stress_ext = extended(wavefields[:, 3:], (("tx", 2), ("ty", 3)), 2)
    acceleration = accelerate(stress_ext, buoyancy, margin, (0, 0, 0))
    velocity = wavefields[:, :3] + time_step * acceleration
    velocity_ext = extended(velocity, (("tx", 2), ("ty", 3)), 2)
    strain = strain_rates(velocity_ext, margin)
    stress = new_stress(wavefields[:, 3:], strain, lame_lambda, shear_modulus)
    local_terms = jnp.sum(
        image_terms(
            strain[:shot_count],
            stress[shot_count:],
            acceleration[:shot_count],
            velocity[shot_count:],
        ),
        axis=0,
    )
    gradient = lax.psum(local_terms, "shot")
    stepped = jnp.concatenate([velocity, stress], axis=1)
    return (stepped[:shot_count], stepped[shot_count:], gradient)


def solution(mesh):
    return jax.shard_map(
        body,
        mesh=mesh,
        in_specs=(
            P("shot", None, "tx", "ty", None),
            P("shot", None, "tx", "ty", None),
            P("tx", "ty", None),
            P("tx", "ty", None),
            P("tx", "ty", None),
            P("shot"),
            P("shot"),
            P("shot", None),
            P("shot", None),
        ),
        out_specs=(
            P("shot", None, "tx", "ty", None),
            P("shot", None, "tx", "ty", None),
            P(None, "tx", "ty", None),
        ),
        check_vma=False,
    )
```

profile of v0, /device:TPU:1, one launch (start us, length us, event | category | flops | bytes accessed | tf_op | source)
XLA Modules:
  0.0 155.1 jit_solution(6553573474216581453)
XLA Ops:
  8.6 0.7 and_select_fusion
  9.4 0.1 reshape.277
  9.5 0.1 broadcast_multiply_fusion.2
  9.6 1.1 fusion.53
  10.6 1.8 %fusion.168 = (f32[1,3,16,16,128]{4,3,2,1,0:T(8,128)S(1)}, f32[1,3,16,16,128]{4,3,2,1,0:T(8,128)S(1)}, f32[1,3,16,16,128]{4,3,2,1,0:T(8,128)S(1)}, f32[1,3,16,16...) fusion(f32[1,9,16,16,128]{4,3,2,1,0:T(8,128)} %param.9, ...), kind=kLoop, calls=%fused_computation.264 | loop fusion | flops 196608 | bytes 4980736 | tf_op jit(solution)/shard_map/vmap()/slice | solution.py:165
  12.5 4.0 %collective-permute-start = (f32[2,6,2,16,128]{4,3,2,1,0:T(8,128)S(1)}, f32[2,6,2,16,128]{4,3,2,1,0:T(8,128)S(1)}, u32[]{:S(2)}, u32[]{:S(2)}) collective-permute-start(f32[2,6,2,16,128]{4,3,2,1,0:T(8,128)S(1)} %get-tuple-element.25), channel_id=1, source_target_pairs={{0,32},{32,64},{64,96},{96,128},{128,160},{160,192},{192,224},{1,3... | collective-permute-start | bytes 589832 | tf_op jit(solution)/shard_map/ppermute | solution.py:18
  16.5 1.3 collective-permute-start.1
  17.8 0.2 maximum_maximum_fusion
  18.0 0.1 slice.469
  18.1 1.0 collective-permute-done
  19.1 3.8 %collective-permute-done.1 = f32[2,6,2,16,128]{4,3,2,1,0:T(8,128)S(1)} collective-permute-done((f32[2,6,2,16,128]{4,3,2,1,0:T(8,128)S(1)}, f32[2,6,2,16,128]{4,3,2,1,0:T(8,128)S(1)}, u32[]{:S(2)}, u32[]{:S(2)}) %collective-permute-start.1) | collective-permute-done | bytes 196640 | tf_op jit(solution)/shard_map/ppermute | solution.py:19
  22.9 0.2 pad_maximum_fusion.6
  23.1 4.1 %collective-permute-start.2 = (f32[2,6,20,2,128]{4,3,2,1,0:T(2,128)S(1)}, f32[2,6,20,2,128]{4,3,2,1,0:T(2,128)S(1)}, u32[]{:S(2)}, u32[]{:S(2)}) collective-permute-start(f32[2,6,20,2,128]{4,3,2,1,0:T(2,128)S(1)} %get-tuple-element.27), channel_id=1, source_target_pairs={{0,1},{1,2},{2,3},{3,4},{4,5},{5,6},{6,7},{7,8},{8,9},{9,10},{10,1... | collective-permute-start | bytes 737288 | tf_op jit(solution)/shard_map/ppermute | solution.py:18
  27.2 1.3 collective-permute-start.3
  28.5 1.7 %collective-permute-done.2 = f32[2,6,20,2,128]{4,3,2,1,0:T(2,128)S(1)} collective-permute-done((f32[2,6,20,2,128]{4,3,2,1,0:T(2,128)S(1)}, f32[2,6,20,2,128]{4,3,2,1,0:T(2,128)S(1)}, u32[]{:S(2)}, u32[]{:S(2)}) %collective-permute-start.2) | collective-permute-done | bytes 245792 | tf_op jit(solution)/shard_map/ppermute | solution.py:18
  30.3 3.8 %collective-permute-done.3 = f32[2,6,20,2,128]{4,3,2,1,0:T(2,128)S(1)} collective-permute-done((f32[2,6,20,2,128]{4,3,2,1,0:T(2,128)S(1)}, f32[2,6,20,2,128]{4,3,2,1,0:T(2,128)S(1)}, u32[]{:S(2)}, u32[]{:S(2)}) %collective-permute-start.3) | collective-permute-done | bytes 245792 | tf_op jit(solution)/shard_map/ppermute | solution.py:19
  34.1 0.4 pad_maximum_fusion
  34.6 0.2 slice_bitcast_fusion.10
  34.8 0.5 fusion.4
  35.2 0.5 fusion.2
  35.7 0.5 fusion.3
  36.2 0.1 copy_add_fusion
  36.3 0.1 maximum_multiply_fusion
  36.4 3.2 %collective-permute-start.4 = (f32[2,3,2,16,128]{4,3,2,0,1:T(8,128)S(1)}, f32[2,3,2,16,128]{4,3,2,0,1:T(8,128)S(1)}, u32[]{:S(2)}, u32[]{:S(2)}) collective-permute-start(f32[2,3,2,16,128]{4,3,2,0,1:T(8,128)S(1)} %get-tuple-element.40), channel_id=1, source_target_pairs={{0,32},{32,64},{64,96},{96,128},{128,160},{160,192},{192,224},{1,3... | collective-permute-start | bytes 294920 | tf_op jit(solution)/shard_map/ppermute | solution.py:18
  39.6 1.3 collective-permute-start.5
  41.0 0.3 collective-permute-done.4
  41.2 15.9 %collective-permute-done.5 = f32[2,3,2,16,128]{4,3,2,0,1:T(8,128)S(1)} collective-permute-done((f32[2,3,2,16,128]{4,3,2,0,1:T(8,128)S(1)}, f32[2,3,2,16,128]{4,3,2,0,1:T(8,128)S(1)}, u32[]{:S(2)}, u32[]{:S(2)}) %collective-permute-start.5) | collective-permute-done | bytes 98336 | tf_op jit(solution)/shard_map/ppermute | solution.py:19
  57.2 0.1 pad_maximum_fusion.9
  57.3 3.1 %collective-permute-start.6 = (f32[2,3,20,2,128]{4,3,2,0,1:T(2,128)S(1)}, f32[2,3,20,2,128]{4,3,2,0,1:T(2,128)S(1)}, u32[]{:S(2)}, u32[]{:S(2)}) collective-permute-start(f32[2,3,20,2,128]{4,3,2,0,1:T(2,128)S(1)} %get-tuple-element.38), channel_id=1, source_target_pairs={{0,1},{1,2},{2,3},{3,4},{4,5},{5,6},{6,7},{7,8},{8,9},{9,10},{10,1... | collective-permute-start | bytes 368648 | tf_op jit(solution)/shard_map/ppermute | solution.py:18
  60.4 1.3 collective-permute-start.7
  61.7 0.5 collective-permute-done.6
  62.2 3.8 %collective-permute-done.7 = f32[2,3,20,2,128]{4,3,2,0,1:T(2,128)S(1)} collective-permute-done((f32[2,3,20,2,128]{4,3,2,0,1:T(2,128)S(1)}, f32[2,3,20,2,128]{4,3,2,0,1:T(2,128)S(1)}, u32[]{:S(2)}, u32[]{:S(2)}) %collective-permute-start.7) | collective-permute-done | bytes 122912 | tf_op jit(solution)/shard_map/ppermute | solution.py:19
  66.0 0.2 pad_maximum_fusion.2
  66.2 0.1 slice_bitcast_fusion.4
  66.4 0.1 bitcast_dynamic-update-slice_fusion.1
  66.5 0.4 bitcast_dynamic-update-slice_fusion
  66.9 0.4 copy-done.1
  67.4 0.2 slice_add_fusion
  67.6 0.2 constant_dynamic-update-slice_fusion.2
  67.8 0.4 constant_dynamic-update-slice_fusion.1
  68.2 0.4 constant_dynamic-update-slice_fusion
  68.6 0.1 fusion.9
  68.8 0.1 fusion.6
  68.9 0.8 maximum_bitcast_fusion
  69.7 0.2 pad_maximum_fusion.1
  69.9 1.6 %slice_bitcast_fusion = (f32[1,9,16,16,128]{4,3,2,1,0:T(8,128)}, f32[1,9,16,16,128]{4,3,2,1,0:T(8,128)}) fusion(f32[2,9,16,16,128]{4,3,2,0,1:T(8,128)S(1)} %pad_maximum_fusion.1), kind=kLoop, calls=%fused_computation.4 | loop fusion | bytes 4718592
  71.4 75.1 %all-reduce.2.cloned.1.call-done = f32[3,16,16,128]{3,2,1,0:T(8,128)} async-done(((f32[3,16,16,128]{3,2,1,0:T(8,128)}), f32[3,16,16,128]{3,2,1,0:T(8,128)}) %all-reduce.2.cloned.1.call-update) | async-done | bytes 393232 | tf_op jit(solution)/shard_map/psum | solution.py:205
  146.5 1.8 %copy.46 = f32[3,16,16,128]{3,2,1,0:T(8,128)} copy(f32[3,16,16,128]{3,2,1,0:T(8,128)} %all-reduce.2.cloned.1.call-done) | data formatting | bytes 786432
  (21 shorter events, 0.4 us)
Async XLA Ops:
  7.2 139.3 %all-reduce.2.cloned.1.call-start = ((), (), s32[]{:S(2)}) async-start(), calls=%async_computation | async-start | bytes 786432 | tf_op jit(solution)/shard_map/psum | solution.py:205
  12.5 6.6 %collective-permute-start = (f32[2,6,2,16,128]{4,3,2,1,0:T(8,128)S(1)}, f32[2,6,2,16,128]{4,3,2,1,0:T(8,128)S(1)}, u32[]{:S(2)}, u32[]{:S(2)}) collective-permute-start(f32[2,6,2,16,128]{4,3,2,1,0:T(8,128)S(1)} %get-tuple-element.25), channel_id=1, source_target_pairs={{0,32},{32,64},{64,96},{96,128},{128,160},{160,192},{192,224},{1,3... | collective-permute-start | bytes 589832 | tf_op jit(solution)/shard_map/ppermute | solution.py:18
  16.5 6.4 %collective-permute-start.1 = (f32[2,6,2,16,128]{4,3,2,1,0:T(8,128)S(1)}, f32[2,6,2,16,128]{4,3,2,1,0:T(8,128)S(1)}, u32[]{:S(2)}, u32[]{:S(2)}) collective-permute-start(f32[2,6,2,16,128]{4,3,2,1,0:T(8,128)S(1)} %get-tuple-element.26), channel_id=1, source_target_pairs={{32,0},{64,32},{96,64},{128,96},{160,128},{192,160},{224,192},{33,... | collective-permute-start | bytes 589832 | tf_op jit(solution)/shard_map/ppermute | solution.py:19
  18.1 10.4 %copy-start.2 = (f32[16,16,128]{2,1,0:T(8,128)S(1)}, f32[16,16,128]{2,1,0:T(8,128)}, u32[]{:S(2)}) copy-start(f32[16,16,128]{2,1,0:T(8,128)} %param.13) | copy-start | bytes 393220
  18.1 10.4 %copy-start = (f32[16,16,128]{2,1,0:T(8,128)S(1)}, f32[16,16,128]{2,1,0:T(8,128)}, u32[]{:S(2)}) copy-start(f32[16,16,128]{2,1,0:T(8,128)} %param.12) | copy-start | bytes 393220
  23.1 7.2 %collective-permute-start.2 = (f32[2,6,20,2,128]{4,3,2,1,0:T(2,128)S(1)}, f32[2,6,20,2,128]{4,3,2,1,0:T(2,128)S(1)}, u32[]{:S(2)}, u32[]{:S(2)}) collective-permute-start(f32[2,6,20,2,128]{4,3,2,1,0:T(2,128)S(1)} %get-tuple-element.27), channel_id=1, source_target_pairs={{0,1},{1,2},{2,3},{3,4},{4,5},{5,6},{6,7},{7,8},{8,9},{9,10},{10,1... | collective-permute-start | bytes 737288 | tf_op jit(solution)/shard_map/ppermute | solution.py:18
  27.2 6.9 %collective-permute-start.3 = (f32[2,6,20,2,128]{4,3,2,1,0:T(2,128)S(1)}, f32[2,6,20,2,128]{4,3,2,1,0:T(2,128)S(1)}, u32[]{:S(2)}, u32[]{:S(2)}) collective-permute-start(f32[2,6,20,2,128]{4,3,2,1,0:T(2,128)S(1)} %get-tuple-element.28), channel_id=1, source_target_pairs={{1,0},{2,1},{3,2},{4,3},{5,4},{6,5},{7,6},{8,7},{9,8},{10,9},{11,1... | collective-permute-start | bytes 737288 | tf_op jit(solution)/shard_map/ppermute | solution.py:19
  36.4 4.8 %collective-permute-start.4 = (f32[2,3,2,16,128]{4,3,2,0,1:T(8,128)S(1)}, f32[2,3,2,16,128]{4,3,2,0,1:T(8,128)S(1)}, u32[]{:S(2)}, u32[]{:S(2)}) collective-permute-start(f32[2,3,2,16,128]{4,3,2,0,1:T(8,128)S(1)} %get-tuple-element.40), channel_id=1, source_target_pairs={{0,32},{32,64},{64,96},{96,128},{128,160},{160,192},{192,224},{1,3... | collective-permute-start | bytes 294920 | tf_op jit(solution)/shard_map/ppermute | solution.py:18
  39.6 17.5 %collective-permute-start.5 = (f32[2,3,2,16,128]{4,3,2,0,1:T(8,128)S(1)}, f32[2,3,2,16,128]{4,3,2,0,1:T(8,128)S(1)}, u32[]{:S(2)}, u32[]{:S(2)}) collective-permute-start(f32[2,3,2,16,128]{4,3,2,0,1:T(8,128)S(1)} %get-tuple-element.41), channel_id=1, source_target_pairs={{32,0},{64,32},{96,64},{128,96},{160,128},{192,160},{224,192},{33,... | collective-permute-start | bytes 294920 | tf_op jit(solution)/shard_map/ppermute | solution.py:19
  57.3 5.0 %collective-permute-start.6 = (f32[2,3,20,2,128]{4,3,2,0,1:T(2,128)S(1)}, f32[2,3,20,2,128]{4,3,2,0,1:T(2,128)S(1)}, u32[]{:S(2)}, u32[]{:S(2)}) collective-permute-start(f32[2,3,20,2,128]{4,3,2,0,1:T(2,128)S(1)} %get-tuple-element.38), channel_id=1, source_target_pairs={{0,1},{1,2},{2,3},{3,4},{4,5},{5,6},{6,7},{7,8},{8,9},{9,10},{10,1... | collective-permute-start | bytes 368648 | tf_op jit(solution)/shard_map/ppermute | solution.py:18
  60.4 5.6 %collective-permute-start.7 = (f32[2,3,20,2,128]{4,3,2,0,1:T(2,128)S(1)}, f32[2,3,20,2,128]{4,3,2,0,1:T(2,128)S(1)}, u32[]{:S(2)}, u32[]{:S(2)}) collective-permute-start(f32[2,3,20,2,128]{4,3,2,0,1:T(2,128)S(1)} %get-tuple-element.39), channel_id=1, source_target_pairs={{1,0},{2,1},{3,2},{4,3},{5,4},{6,5},{7,6},{8,7},{9,8},{10,9},{11,1... | collective-permute-start | bytes 368648 | tf_op jit(solution)/shard_map/ppermute | solution.py:19
  66.4 0.9 copy-start.1
Sparse Core Ops, SparseCore 0:
  69.8 76.6 all-reduce.1
where the time goes:
time: 156 us; the launch traced here: 155 us
  waiting for transfers between devices  106 us (68%)
  starting transfers between devices  19.6 us (13%)
  between operations  15.8 us (10%)
  other arithmetic  5.89 us (4%)
  local copies, waits for them, and re-layouts  4.22 us (3%)
  matrix products  3.63 us (2%)
    psum x1, waiting for transfers between devices, body(): gradient = lax.psum(local_terms, 'shot')  75.1 us
    ppermute x4, waiting for transfers between devices, extended(): after = lax.ppermute(initial, axis, down)  27.4 us
    ppermute x4, starting transfers between devices, extended(): before = lax.ppermute(last, axis, up)  14.4 us
    ppermute x4, starting transfers between devices, extended(): after = lax.ppermute(initial, axis, down)  5.17 us
    unnamed x8, local copies, waits for them, and re-layouts  3.73 us
    ppermute x4, waiting for transfers between devices, extended(): before = lax.ppermute(last, axis, up)  3.5 us
  transfers between devices with their start and end apart: 9, of which 9 were waited for; matrix products, arithmetic and copies ran while one was open for 1% of the time, Pallas kernels for 0%

commit v1 on v0

--- a/solution.py
+++ b/solution.py
@@ -202,7 +202,8 @@
         ),
         axis=0,
     )
-    gradient = lax.psum(local_terms, "shot")
+    shards = lax.all_gather(local_terms, "shot")
+    gradient = jnp.sum(shards, axis=0)
     stepped = jnp.concatenate([velocity, stress], axis=1)
     return (stepped[:shot_count], stepped[shot_count:], gradient)
 

time: 156 us -> 112 us (0.72)
  the two profiles are of different devices: /device:TPU:1 before, /device:TPU:31 now
where the time goes in v1:
time: 112 us
  starting transfers between devices  45.7 us (41%)
  waiting for transfers between devices  42.3 us (38%)
  blocking collectives  9.13 us (8%)
  other arithmetic  5.97 us (5%)
  matrix products  3.63 us (3%)
  local copies, waits for them, and re-layouts  2.47 us (2%)
  between operations  2.41 us (2%)
    ppermute x4, waiting for transfers between devices, extended(): after = lax.ppermute(initial, axis, down)  39.2 us
    ppermute x4, starting transfers between devices, extended(): before = lax.ppermute(last, axis, up)  36.5 us
    all_gather x1, blocking collectives, body(): shards = lax.all_gather(local_terms, 'shot')  9.13 us
    ppermute x4, starting transfers between devices, extended(): after = lax.ppermute(initial, axis, down)  9.12 us
    ppermute x4, waiting for transfers between devices, extended(): before = lax.ppermute(last, axis, up)  3.08 us
    dot_general x6, matrix products, derive(): jnp.einsum('...k,ki->...i', core, depth_table(core.shape[-1], upward), pr...  2.58 us
  transfers between devices with their start and end apart: 8, of which 7 were waited for; matrix products, arithmetic and copies ran while one was open for 0% of the time, Pallas kernels for 0%

profile of v1, /device:TPU:31, one launch (start us, length us, event | category | flops | bytes accessed | tf_op | source)
XLA Modules:
  0.0 111.6 jit_solution(1189264514498616408)
XLA Ops:
  2.1 0.7 and_select_fusion
  2.8 0.1 reshape.278
  2.9 0.1 broadcast_multiply_fusion.2
  3.0 1.1 fusion.53
  4.0 1.8 %fusion.168 = (f32[1,3,16,16,128]{4,3,2,1,0:T(8,128)S(1)}, f32[1,3,16,16,128]{4,3,2,1,0:T(8,128)S(1)}, f32[1,3,16,16,128]{4,3,2,1,0:T(8,128)S(1)}, f32[1,3,16,16...) fusion(f32[1,9,16,16,128]{4,3,2,1,0:T(8,128)} %param.9, ...), kind=kLoop, calls=%fused_computation.264 | loop fusion | flops 196608 | bytes 4980736 | tf_op jit(solution)/shard_map/vmap()/slice | solution.py:165
  5.9 15.1 %collective-permute-start = (f32[2,6,2,16,128]{4,3,2,1,0:T(8,128)S(1)}, f32[2,6,2,16,128]{4,3,2,1,0:T(8,128)S(1)}, u32[]{:S(2)}, u32[]{:S(2)}) collective-permute-start(f32[2,6,2,16,128]{4,3,2,1,0:T(8,128)S(1)} %get-tuple-element.28), channel_id=1, source_target_pairs={{0,32},{32,64},{64,96},{96,128},{128,160},{160,192},{192,224},{1,3... | collective-permute-start | bytes 589832 | tf_op jit(solution)/shard_map/ppermute | solution.py:18
  21.0 1.9 %collective-permute-start.1 = (f32[2,6,2,16,128]{4,3,2,1,0:T(8,128)S(1)}, f32[2,6,2,16,128]{4,3,2,1,0:T(8,128)S(1)}, u32[]{:S(2)}, u32[]{:S(2)}) collective-permute-start(f32[2,6,2,16,128]{4,3,2,1,0:T(8,128)S(1)} %get-tuple-element.29), channel_id=1, source_target_pairs={{32,0},{64,32},{96,64},{128,96},{160,128},{192,160},{224,192},{33,... | collective-permute-start | bytes 589832 | tf_op jit(solution)/shard_map/ppermute | solution.py:19
  22.9 0.2 maximum_maximum_fusion
  23.1 0.1 slice.469
  23.2 1.3 %collective-permute-done = f32[2,6,2,16,128]{4,3,2,1,0:T(8,128)S(1)} collective-permute-done((f32[2,6,2,16,128]{4,3,2,1,0:T(8,128)S(1)}, f32[2,6,2,16,128]{4,3,2,1,0:T(8,128)S(1)}, u32[]{:S(2)}, u32[]{:S(2)}) %collective-permute-start) | collective-permute-done | bytes 196640 | tf_op jit(solution)/shard_map/ppermute | solution.py:18
  24.5 14.6 %collective-permute-done.1 = f32[2,6,2,16,128]{4,3,2,1,0:T(8,128)S(1)} collective-permute-done((f32[2,6,2,16,128]{4,3,2,1,0:T(8,128)S(1)}, f32[2,6,2,16,128]{4,3,2,1,0:T(8,128)S(1)}, u32[]{:S(2)}, u32[]{:S(2)}) %collective-permute-start.1) | collective-permute-done | bytes 196640 | tf_op jit(solution)/shard_map/ppermute | solution.py:19
  39.2 0.2 pad_maximum_fusion.7
  39.3 15.6 %collective-permute-start.2 = (f32[2,6,20,2,128]{4,3,2,1,0:T(2,128)S(1)}, f32[2,6,20,2,128]{4,3,2,1,0:T(2,128)S(1)}, u32[]{:S(2)}, u32[]{:S(2)}) collective-permute-start(f32[2,6,20,2,128]{4,3,2,1,0:T(2,128)S(1)} %get-tuple-element.30), channel_id=1, source_target_pairs={{0,1},{1,2},{2,3},{3,4},{4,5},{5,6},{6,7},{7,8},{8,9},{9,10},{10,1... | collective-permute-start | bytes 737288 | tf_op jit(solution)/shard_map/ppermute | solution.py:18
  54.9 1.9 %collective-permute-start.3 = (f32[2,6,20,2,128]{4,3,2,1,0:T(2,128)S(1)}, f32[2,6,20,2,128]{4,3,2,1,0:T(2,128)S(1)}, u32[]{:S(2)}, u32[]{:S(2)}) collective-permute-start(f32[2,6,20,2,128]{4,3,2,1,0:T(2,128)S(1)} %get-tuple-element.31), channel_id=1, source_target_pairs={{1,0},{2,1},{3,2},{4,3},{5,4},{6,5},{7,6},{8,7},{9,8},{10,9},{11,1... | collective-permute-start | bytes 737288 | tf_op jit(solution)/shard_map/ppermute | solution.py:19
  57.0 1.7 %collective-permute-done.2 = f32[2,6,20,2,128]{4,3,2,1,0:T(2,128)S(1)} collective-permute-done((f32[2,6,20,2,128]{4,3,2,1,0:T(2,128)S(1)}, f32[2,6,20,2,128]{4,3,2,1,0:T(2,128)S(1)}, u32[]{:S(2)}, u32[]{:S(2)}) %collective-permute-start.2) | collective-permute-done | bytes 245792 | tf_op jit(solution)/shard_map/ppermute | solution.py:18
  58.7 5.9 %collective-permute-done.3 = f32[2,6,20,2,128]{4,3,2,1,0:T(2,128)S(1)} collective-permute-done((f32[2,6,20,2,128]{4,3,2,1,0:T(2,128)S(1)}, f32[2,6,20,2,128]{4,3,2,1,0:T(2,128)S(1)}, u32[]{:S(2)}, u32[]{:S(2)}) %collective-permute-start.3) | collective-permute-done | bytes 245792 | tf_op jit(solution)/shard_map/ppermute | solution.py:19
  64.6 0.4 pad_maximum_fusion
  65.0 0.2 slice_bitcast_fusion.10
  65.3 0.5 fusion.4
  65.7 0.5 fusion.2
  66.2 0.5 fusion.3
  66.7 0.1 copy_add_fusion
  66.8 0.1 maximum_multiply_fusion
  66.9 1.9 %collective-permute-start.4 = (f32[2,3,2,16,128]{4,3,2,0,1:T(8,128)S(1)}, f32[2,3,2,16,128]{4,3,2,0,1:T(8,128)S(1)}, u32[]{:S(2)}, u32[]{:S(2)}) collective-permute-start(f32[2,3,2,16,128]{4,3,2,0,1:T(8,128)S(1)} %get-tuple-element.43), channel_id=1, source_target_pairs={{0,32},{32,64},{64,96},{96,128},{128,160},{160,192},{192,224},{1,3... | collective-permute-start | bytes 294920 | tf_op jit(solution)/shard_map/ppermute | solution.py:18
  68.9 3.4 %collective-permute-start.5 = (f32[2,3,2,16,128]{4,3,2,0,1:T(8,128)S(1)}, f32[2,3,2,16,128]{4,3,2,0,1:T(8,128)S(1)}, u32[]{:S(2)}, u32[]{:S(2)}) collective-permute-start(f32[2,3,2,16,128]{4,3,2,0,1:T(8,128)S(1)} %get-tuple-element.44), channel_id=1, source_target_pairs={{32,0},{64,32},{96,64},{128,96},{160,128},{192,160},{224,192},{33,... | collective-permute-start | bytes 294920 | tf_op jit(solution)/shard_map/ppermute | solution.py:19
  72.3 12.9 %collective-permute-done.5 = f32[2,3,2,16,128]{4,3,2,0,1:T(8,128)S(1)} collective-permute-done((f32[2,3,2,16,128]{4,3,2,0,1:T(8,128)S(1)}, f32[2,3,2,16,128]{4,3,2,0,1:T(8,128)S(1)}, u32[]{:S(2)}, u32[]{:S(2)}) %collective-permute-start.5) | collective-permute-done | bytes 98336 | tf_op jit(solution)/shard_map/ppermute | solution.py:19
  85.2 0.1 pad_maximum_fusion.10
  85.3 3.9 %collective-permute-start.6 = (f32[2,3,20,2,128]{4,3,2,0,1:T(2,128)S(1)}, f32[2,3,20,2,128]{4,3,2,0,1:T(2,128)S(1)}, u32[]{:S(2)}, u32[]{:S(2)}) collective-permute-start(f32[2,3,20,2,128]{4,3,2,0,1:T(2,128)S(1)} %get-tuple-element.41), channel_id=1, source_target_pairs={{0,1},{1,2},{2,3},{3,4},{4,5},{5,6},{6,7},{7,8},{8,9},{9,10},{10,1... | collective-permute-start | bytes 368648 | tf_op jit(solution)/shard_map/ppermute | solution.py:18
  89.2 1.9 %collective-permute-start.7 = (f32[2,3,20,2,128]{4,3,2,0,1:T(2,128)S(1)}, f32[2,3,20,2,128]{4,3,2,0,1:T(2,128)S(1)}, u32[]{:S(2)}, u32[]{:S(2)}) collective-permute-start(f32[2,3,20,2,128]{4,3,2,0,1:T(2,128)S(1)} %get-tuple-element.42), channel_id=1, source_target_pairs={{1,0},{2,1},{3,2},{4,3},{5,4},{6,5},{7,6},{8,7},{9,8},{10,9},{11,1... | collective-permute-start | bytes 368648 | tf_op jit(solution)/shard_map/ppermute | solution.py:19
  91.2 0.1 collective-permute-done.6
  91.2 5.7 %collective-permute-done.7 = f32[2,3,20,2,128]{4,3,2,0,1:T(2,128)S(1)} collective-permute-done((f32[2,3,20,2,128]{4,3,2,0,1:T(2,128)S(1)}, f32[2,3,20,2,128]{4,3,2,0,1:T(2,128)S(1)}, u32[]{:S(2)}, u32[]{:S(2)}) %collective-permute-start.7) | collective-permute-done | bytes 122912 | tf_op jit(solution)/shard_map/ppermute | solution.py:19
  96.9 0.2 pad_maximum_fusion.2
  97.2 0.1 slice_bitcast_fusion.4
  97.3 0.1 bitcast_dynamic-update-slice_fusion.2
  97.4 0.1 bitcast_dynamic-update-slice_fusion.1
  97.5 0.4 bitcast_dynamic-update-slice_fusion
  97.9 0.4 copy-done.1
  98.3 0.1 add_multiply_fusion
  98.3 0.2 slice_add_fusion
  98.6 0.2 constant_dynamic-update-slice_fusion.2
  98.8 0.4 constant_dynamic-update-slice_fusion.1
  99.2 0.4 constant_dynamic-update-slice_fusion
  99.6 0.1 fusion.9
  99.7 0.2 pad_maximum_fusion.1
  99.9 0.1 fusion.6
  100.1 1.6 %slice_bitcast_fusion = (f32[1,9,16,16,128]{4,3,2,1,0:T(8,128)}, f32[1,9,16,16,128]{4,3,2,1,0:T(8,128)}) fusion(f32[2,9,16,16,128]{4,3,2,0,1:T(8,128)S(1)} %pad_maximum_fusion.1), kind=kLoop, calls=%fused_computation.4 | loop fusion | bytes 4718592
  101.6 9.1 %all_gather.4 = f32[2,3,16,16,128]{4,3,2,1,0:T(8,128)S(1)} all-gather(f32[1,3,16,16,128]{4,3,2,1,0:T(8,128)S(1)} %pad_maximum_fusion.4), channel_id=1, replica_groups=mesh['shot'=2,'tx'=8,'ty'=32] {'shot'}, dimensions={0}, use_global_device_ids=true | all-gather | bytes 1179648 | tf_op jit(solution)/shard_map/all_gather | solution.py:205
  110.8 0.8 reduce_sum.33
  (19 shorter events, 0.3 us)
Async XLA Ops:
  5.9 18.7 %collective-permute-start = (f32[2,6,2,16,128]{4,3,2,1,0:T(8,128)S(1)}, f32[2,6,2,16,128]{4,3,2,1,0:T(8,128)S(1)}, u32[]{:S(2)}, u32[]{:S(2)}) collective-permute-start(f32[2,6,2,16,128]{4,3,2,1,0:T(8,128)S(1)} %get-tuple-element.28), channel_id=1, source_target_pairs={{0,32},{32,64},{64,96},{96,128},{128,160},{160,192},{192,224},{1,3... | collective-permute-start | bytes 589832 | tf_op jit(solution)/shard_map/ppermute | solution.py:18
  21.0 18.2 %collective-permute-start.1 = (f32[2,6,2,16,128]{4,3,2,1,0:T(8,128)S(1)}, f32[2,6,2,16,128]{4,3,2,1,0:T(8,128)S(1)}, u32[]{:S(2)}, u32[]{:S(2)}) collective-permute-start(f32[2,6,2,16,128]{4,3,2,1,0:T(8,128)S(1)} %get-tuple-element.29), channel_id=1, source_target_pairs={{32,0},{64,32},{96,64},{128,96},{160,128},{192,160},{224,192},{33,... | collective-permute-start | bytes 589832 | tf_op jit(solution)/shard_map/ppermute | solution.py:19
  23.2 33.7 %copy-start.2 = (f32[16,16,128]{2,1,0:T(8,128)S(1)}, f32[16,16,128]{2,1,0:T(8,128)}, u32[]{:S(2)}) copy-start(f32[16,16,128]{2,1,0:T(8,128)} %param.13) | copy-start | bytes 393220
  23.2 33.7 %copy-start = (f32[16,16,128]{2,1,0:T(8,128)S(1)}, f32[16,16,128]{2,1,0:T(8,128)}, u32[]{:S(2)}) copy-start(f32[16,16,128]{2,1,0:T(8,128)} %param.12) | copy-start | bytes 393220
  39.3 19.3 %collective-permute-start.2 = (f32[2,6,20,2,128]{4,3,2,1,0:T(2,128)S(1)}, f32[2,6,20,2,128]{4,3,2,1,0:T(2,128)S(1)}, u32[]{:S(2)}, u32[]{:S(2)}) collective-permute-start(f32[2,6,20,2,128]{4,3,2,1,0:T(2,128)S(1)} %get-tuple-element.30), channel_id=1, source_target_pairs={{0,1},{1,2},{2,3},{3,4},{4,5},{5,6},{6,7},{7,8},{8,9},{9,10},{10,1... | collective-permute-start | bytes 737288 | tf_op jit(solution)/shard_map/ppermute | solution.py:18
  54.9 9.7 %collective-permute-start.3 = (f32[2,6,20,2,128]{4,3,2,1,0:T(2,128)S(1)}, f32[2,6,20,2,128]{4,3,2,1,0:T(2,128)S(1)}, u32[]{:S(2)}, u32[]{:S(2)}) collective-permute-start(f32[2,6,20,2,128]{4,3,2,1,0:T(2,128)S(1)} %get-tuple-element.31), channel_id=1, source_target_pairs={{1,0},{2,1},{3,2},{4,3},{5,4},{6,5},{7,6},{8,7},{9,8},{10,9},{11,1... | collective-permute-start | bytes 737288 | tf_op jit(solution)/shard_map/ppermute | solution.py:19
  66.9 5.4 %collective-permute-start.4 = (f32[2,3,2,16,128]{4,3,2,0,1:T(8,128)S(1)}, f32[2,3,2,16,128]{4,3,2,0,1:T(8,128)S(1)}, u32[]{:S(2)}, u32[]{:S(2)}) collective-permute-start(f32[2,3,2,16,128]{4,3,2,0,1:T(8,128)S(1)} %get-tuple-element.43), channel_id=1, source_target_pairs={{0,32},{32,64},{64,96},{96,128},{128,160},{160,192},{192,224},{1,3... | collective-permute-start | bytes 294920 | tf_op jit(solution)/shard_map/ppermute | solution.py:18
  68.9 16.4 %collective-permute-start.5 = (f32[2,3,2,16,128]{4,3,2,0,1:T(8,128)S(1)}, f32[2,3,2,16,128]{4,3,2,0,1:T(8,128)S(1)}, u32[]{:S(2)}, u32[]{:S(2)}) collective-permute-start(f32[2,3,2,16,128]{4,3,2,0,1:T(8,128)S(1)} %get-tuple-element.44), channel_id=1, source_target_pairs={{32,0},{64,32},{96,64},{128,96},{160,128},{192,160},{224,192},{33,... | collective-permute-start | bytes 294920 | tf_op jit(solution)/shard_map/ppermute | solution.py:19
  85.3 5.9 %collective-permute-start.6 = (f32[2,3,20,2,128]{4,3,2,0,1:T(2,128)S(1)}, f32[2,3,20,2,128]{4,3,2,0,1:T(2,128)S(1)}, u32[]{:S(2)}, u32[]{:S(2)}) collective-permute-start(f32[2,3,20,2,128]{4,3,2,0,1:T(2,128)S(1)} %get-tuple-element.41), channel_id=1, source_target_pairs={{0,1},{1,2},{2,3},{3,4},{4,5},{5,6},{6,7},{7,8},{8,9},{9,10},{10,1... | collective-permute-start | bytes 368648 | tf_op jit(solution)/shard_map/ppermute | solution.py:18
  89.2 7.7 %collective-permute-start.7 = (f32[2,3,20,2,128]{4,3,2,0,1:T(2,128)S(1)}, f32[2,3,20,2,128]{4,3,2,0,1:T(2,128)S(1)}, u32[]{:S(2)}, u32[]{:S(2)}) collective-permute-start(f32[2,3,20,2,128]{4,3,2,0,1:T(2,128)S(1)} %get-tuple-element.42), channel_id=1, source_target_pairs={{1,0},{2,1},{3,2},{4,3},{5,4},{6,5},{7,6},{8,7},{9,8},{10,9},{11,1... | collective-permute-start | bytes 368648 | tf_op jit(solution)/shard_map/ppermute | solution.py:19
  97.4 0.9 copy-start.1
